TPU v7x, 512 devices: a whole 4x8x8 slice. The times are simulated.
512 devices in a mesh: row: 16 (over x_lo, y), tm: 8 (over z), head: 4 (over x_hi, core).
Axes of the slice: x: 4 (x_hi: 2, x_lo: 2; x = x_hi * 2 + x_lo), y: 8, z: 8, core: 2. Of those that a mesh axis runs over, the one named last changes fastest.
Arguments:
- stream: bfloat16 [32, 64, 24, 3072], P('tm', 'row'), may hold values from -60 to 60
- qkv1: bfloat16 [32, 64, 24, 3, 1536], P('tm', 'row', None, None, 'head'), may hold values from -40 to 40
- w_out1: bfloat16 [3072, 1536], P(('row', 'tm'), 'head'), may hold values from -0.5 to 0.5
- gain: float32 [3072], replicated, may hold values from 0.3 to 3
- w_qkv2: bfloat16 [3072, 3, 1536], P(('row', 'tm'), None, 'head'), may hold values from -0.8 to 0.8
Outputs:
- updated: bfloat16 [32, 64, 24, 3072], P('tm', 'row', None, 'head')
- layer_two: bfloat16 [32, 64, 24, 1536], P('tm', 'row', None, 'head')
All inputs are finite; a program needn't handle non-finite values.
Results may differ from a plain program's by a relative error of at most 0.033.
Values may be sent and summed in bfloat16 or wider, within the bound.
A program may use at most 64 MiB of HBM per device.

v0:
```python
import jax
import jax.numpy as jnp
from jax import lax
from jax.sharding import PartitionSpec as P

HDIM = 128
WT = 4
WH = 4
WW = 8


EPSILON = 1e-06


def shifted_2(block, axis, distance):
    devices = range(lax.axis_size(axis))
    route = [((i - distance) % len(devices), i) for i in devices]
    return lax.ppermute(block, axis, route)


def windows(array, head_count):
    frames, tile_rows, tile_cols = (array.shape[0], array.shape[1], array.shape[2])
    array = array.reshape(
        frames // WT, WT, tile_rows // WH, WH, tile_cols // WW, WW, head_count, HDIM
    )
    array = array.transpose(0, 2, 4, 6, 1, 3, 5, 7)
    return array.reshape(-1, head_count, WT * WH * WW, HDIM)


def unwindow(array, frames, tile_rows, tile_cols):
    head_count = array.shape[1]
    array = array.reshape(
        frames // WT, tile_rows // WH, tile_cols // WW, head_count, WT, WH, WW, HDIM
    )
    array = array.transpose(0, 4, 1, 5, 2, 6, 3, 7)
    return array.reshape(frames, tile_rows, tile_cols, head_count * HDIM)


def attend(query, keys, values):
    frames, tile_rows, tile_cols, channels = query.shape
    head_count = channels // HDIM
    query_w = windows(query, head_count)
    keys_w = windows(keys, head_count)
    values_w = windows(values, head_count)
    scores = jnp.einsum(
        "nhqd,nhkd->nhqk", query_w, keys_w, preferred_element_type=jnp.float32
    ) * HDIM ** (-0.5)
    largest = jnp.max(scores, axis=-1, keepdims=True)
    weights = jnp.exp(scores - largest)
    probabilities = (weights / jnp.sum(weights, axis=-1, keepdims=True)).astype(jnp.bfloat16)
    attended = jnp.einsum(
        "nhqk,nhkd->nhqd", probabilities, values_w, preferred_element_type=jnp.float32
    ).astype(jnp.bfloat16)
    return unwindow(attended, frames, tile_rows, tile_cols)


def roll_rows(array):
    front_slab = shifted_2(array[:, : WH // 2], "row", -1)
    return jnp.concatenate([array[:, WH // 2 :], front_slab], axis=1)


def roll_frames(array):
    front_slab = shifted_2(array[: WT // 2], "tm", -1)
    return jnp.concatenate([array[WT // 2 :], front_slab], axis=0)


def back_frames(array):
    rear_slab = shifted_2(array[WT - WT // 2 :], "tm", 1)
    return jnp.concatenate([rear_slab, array[: WT - WT // 2]], axis=0)


def back_rows(array):
    rear_slab = shifted_2(array[:, WH - WH // 2 :], "row", 1)
    return jnp.concatenate([rear_slab, array[:, : WH - WH // 2]], axis=1)


def shards(stream, qkv1, w_out1, gain, w_qkv2):
    frames, tile_rows, tile_cols, channels = stream.shape
    token_count = frames * tile_rows * tile_cols
    group_width = qkv1.shape[-1]
    layer_one = attend(qkv1[..., 0, :], qkv1[..., 1, :], qkv1[..., 2, :]).reshape(
        token_count, group_width
    )
    partial_value = lax.dot_general(
        layer_one,
        lax.all_gather(w_out1, ("row", "tm"), axis=0, tiled=True),
        (((1,), (1,)), ((), ())),
        preferred_element_type=jnp.float32,
    )
    share_width = channels // lax.axis_size("head")
    offset = lax.axis_index("head") * share_width
    flat_stream = stream.reshape(token_count, channels)
    full_sum = lax.psum(partial_value.astype(jnp.bfloat16), "head").astype(jnp.float32)
    updated = (flat_stream.astype(jnp.float32) + full_sum).astype(jnp.bfloat16)
    values = updated.astype(jnp.float32)
    meansq = jnp.mean(values * values, axis=-1, keepdims=True)
    normed = (values * lax.rsqrt(meansq + EPSILON) * gain).astype(jnp.bfloat16)
    updated_share = lax.dynamic_slice_in_dim(updated, offset, share_width, 1)
    weight_rows = lax.all_gather(w_qkv2, ("row", "tm"), axis=0, tiled=True)
    row_count = weight_rows.shape[0]
    projected = jnp.dot(
        normed, weight_rows.reshape(row_count, 3 * group_width), preferred_element_type=jnp.float32
    )
    qkv_two = projected.astype(jnp.bfloat16).reshape(frames, tile_rows, tile_cols, 3, group_width)
    shifted = roll_frames(roll_rows(qkv_two))
    attended = attend(shifted[..., 0, :], shifted[..., 1, :], shifted[..., 2, :])
    layer_two = back_rows(back_frames(attended))
    return (updated_share.reshape(frames, tile_rows, tile_cols, share_width), layer_two)


def solution(mesh):
    in_specs = (
        P("tm", "row", None, None),
        P("tm", "row", None, None, "head"),
        P(("row", "tm"), "head"),
        P(),
        P(("row", "tm"), None, "head"),
    )
    out_specs = (P("tm", "row", None, "head"), P("tm", "row", None, "head"))
    return jax.shard_map(shards, mesh=mesh, in_specs=in_specs, out_specs=out_specs, check_vma=False)
```

profile of v0, /device:TPU:4, one launch (start us, length us, event | category | flops | bytes accessed | tf_op | source)
XLA Modules:
  0.0 1347.8 jit_solution(1989076875011394537)
XLA Ops:
  7.2 0.7 all-gather.3.cloned.1.call-update
  7.9 1.3 slice_bitcast_fusion.1
  9.4 0.4 fusion.27
  9.8 0.3 convolution_multiply_fusion.1
  10.2 0.3 convolution_convert_fusion.3
  10.6 592.5 %all-gather.3.cloned.1.call-done = bf16[3072,384]{1,0:T(8,128)(2,1)} async-done(((bf16[24,384]{1,0:T(8,128)(2,1)}), bf16[3072,384]{1,0:T(8,128)(2,1)}) %all-gather.3.cloned.1.call-update) | async-done | bytes 2359312 | tf_op jit(solution)/shard_map/all_gather | solution.py:86
  603.1 4.5 convolution_convert_fusion
  607.7 0.7 all-gather.5.cloned.1.call-update
  608.4 63.8 %all-reduce.2.cloned.1.call-done = bf16[384,3072]{1,0:T(8,128)(2,1)} async-done(((bf16[384,3072]{1,0:T(8,128)(2,1)}), bf16[384,3072]{1,0:T(8,128)(2,1)}) %all-reduce.2.cloned.1.call-update) | async-done | bytes 2359312 | tf_op jit(solution)/shard_map/psum | solution.py:93
  672.3 3.5 fusion.2
  675.8 600.5 %all-gather.5.cloned.1.call-done = bf16[3072,3,384]{2,0,1:T(8,128)(2,1)} async-done(((bf16[24,3,384]{2,0,1:T(8,128)(2,1)}), bf16[3072,3,384]{2,0,1:T(8,128)(2,1)}) %all-gather.5.cloned.1.call-update) | async-done | bytes 7077904 | tf_op jit(solution)/shard_map/all_gather | solution.py:99
  1276.2 10.1 copy.37
  1286.3 7.2 convolution_convert_fusion.1
  1293.5 2.1 reshape.62
  1295.6 0.4 fusion.25
  1296.1 1.9 collective-permute-start
  1298.0 8.3 collective-permute-done
  1306.3 0.2 copy.39
  1306.5 0.8 fusion.13
  1307.4 3.3 collective-permute-start.1
  1310.7 6.9 collective-permute-done.1
  1317.6 0.2 copy.41
  1317.8 1.7 fusion.14
  1319.8 0.4 fusion.28
  1320.2 1.2 convolution_multiply_fusion
  1321.4 1.6 convolution_convert_fusion.2
  1323.1 1.9 collective-permute-start.2
  1325.1 6.3 collective-permute-done.2
  1331.4 1.9 collective-permute-start.3
  1333.3 0.9 constant_dynamic-slice_fusion
  1334.2 6.3 collective-permute-done.3
  1340.5 0.8 fusion.16
  (22 shorter events, 0.9 us)
Async XLA Ops:
  7.2 596.0 %all-gather.3.cloned.1.call-start = ((), (), s32[]{:S(2)}) async-start(), calls=%async_computation | async-start | bytes 2377728 | tf_op jit(solution)/shard_map/all_gather | solution.py:86
  7.9 664.4 %all-reduce.2.cloned.1.call-start = ((), (), s32[]{:S(2)}) async-start(), calls=%async_computation.1 | async-start | bytes 4718592 | tf_op jit(solution)/shard_map/psum | solution.py:93
  607.7 668.5 %all-gather.5.cloned.1.call-start = ((), (), s32[]{:S(2)}) async-start(), calls=%async_computation.2 | async-start | bytes 7133184 | tf_op jit(solution)/shard_map/all_gather | solution.py:99
  675.7 610.6 %copy-start = (f32[3072]{0:T(1024)S(1)}, f32[3072]{0:T(1024)}, u32[]{:S(2)}) copy-start(f32[3072]{0:T(1024)} %param.8) | copy-start | bytes 36868
  1296.1 10.2 collective-permute-start
  1307.4 10.2 collective-permute-start.1
  1323.1 8.2 collective-permute-start.2
  1331.4 9.1 collective-permute-start.3
Sparse Core Ops, SparseCore 0:
  10.1 592.9 all-gather.2
  607.8 64.3 all-reduce.1
  674.4 601.8 all-gather.4
where the time goes:
time: 1350 us
  waiting for transfers between devices  1290 us (96%)
  local copies, waits for them, and re-layouts  16 us (1%)
  matrix products  16 us (1%)
  between operations  14 us (1%)
    all_gather x1, waiting for transfers between devices, shards(): weight_rows = lax.all_gather(w_qkv2, ('row', 'tm'), axis=0, tiled=True)  600 us
    all_gather x1, waiting for transfers between devices, shards(): lax.all_gather(w_out1, ('row', 'tm'), axis=0, tiled=True)  593 us
    psum x1, waiting for transfers between devices, shards(): lax.psum(partial_value.astype(jnp.bfloat16), 'head').astype(jnp.float32)  63.8 us
    ppermute x4, waiting for transfers between devices, shifted_2(): return lax.ppermute(block, axis, route)  27.7 us
  transfers between devices with their start and end apart: 7, of which 7 were waited for; matrix products, arithmetic and copies ran while one was open for 1% of the time, Pallas kernels for 0%

commit v1 on v0

v1 whole, which is shorter than its diff:
```python
import jax
import jax.numpy as jnp
from jax import lax
from jax.experimental import pallas as pl
from jax.experimental.pallas import tpu as pltpu
from jax.sharding import PartitionSpec as P

MESH = pl.DeviceIdType.MESH
HDIM = 128
EPSILON = 1e-06
TOKENS = 384
SHARE = 768
GROUP = 384
WIDE = 1152
CHUNKS = 2
PART = TOKENS // CHUNKS
BF = jnp.bfloat16
F32 = jnp.float32

FIRST = (0, 8)
SECOND = (16, 32)
PAIR = 48
CORE_PART = 49
SUM_X = 51
SHARE_X = SUM_X + CHUNKS
SHARE_CORE = SHARE_X + CHUNKS
RELAY = SHARE_CORE + CHUNKS
HALO = RELAY + CHUNKS
BACK = HALO + 3
N_SEM = BACK + 3


def softmax_attend(q, k, v):
    scores = lax.dot_general(
        q, k, (((1,), (1,)), ((), ())), preferred_element_type=F32
    ) * HDIM ** (-0.5)
    largest = jnp.max(scores, axis=-1, keepdims=True)
    weights = jnp.exp(scores - largest)
    probabilities = (weights / jnp.sum(weights, axis=-1, keepdims=True)).astype(BF)
    return jnp.dot(probabilities, v, preferred_element_type=F32)


def kernel(
    qw, wo, wq, gain, stream, upd_out, two_out,
    own, other, ga, gb, w1, w2, l1f, l1, ps, pr, qs, xr, xf, st, ub, nb, acc, pj, hq, x2, o2, ob, lb,
    ssem, rsem, lsem,
):
    row = lax.axis_index("row")
    z = lax.axis_index("tm")
    head = lax.axis_index("head")
    xl, y = row // 8, row % 8
    xh, c = head // 2, head % 2

    def first(d):
        return (xl * 8 + (y + c * (d + 8)) % 8, (z + (1 - c) * (d + 8)) % 8, head)

    def second(d):
        return (xl * 8 + (y + (1 - c) * (d + 8)) % 8, (z + c * (d + 8)) % 8, head)

    p0 = (1 - c) * z + c * y
    s0 = (1 - c) * y + c * z
    pair_dev = ((row + 8) % 16, z, head)
    core_dev = (row, z, xh * 2 + (1 - c))
    x_dev = (row, z, (head + 2) % 4)
    row_m, row_p = (row + 15) % 16, (row + 1) % 16
    z_m, z_p = (z + 7) % 8, (z + 1) % 8
    halo_to = ((row_m, z, head), (row, z_m, head), (row_m, z_m, head))
    halo_from = ((row_p, z, head), (row, z_p, head), (row_p, z_p, head))

    barrier = pltpu.get_barrier_semaphore()
    greet = (first(1), first(-1), second(1), second(-1), pair_dev, core_dev, x_dev) + halo_to + halo_from
    for device in greet:
        pl.semaphore_signal(barrier, inc=1, device_id=device, device_id_type=MESH)
    pl.semaphore_wait(barrier, len(greet))

    sent = []

    def send(src, dst, k, device):
        copy = pltpu.make_async_remote_copy(
            src_ref=src, dst_ref=dst, send_sem=ssem.at[k], recv_sem=rsem.at[k],
            device_id=device, device_id_type=MESH,
        )
        copy.start()
        sent.append(copy)

    def arrive(dst, k, device):
        pltpu.make_async_remote_copy(
            src_ref=dst, dst_ref=dst, send_sem=ssem.at[k], recv_sem=rsem.at[k],
            device_id=device, device_id_type=MESH,
        ).wait_recv()

    stream_in = pltpu.make_async_copy(
        stream.at[:, pl.ds(pl.multiple_of(head * SHARE, SHARE), SHARE)], st, lsem.at[0]
    )
    stream_in.start()

    mine = jnp.concatenate([wo[...].astype(F32), wq[...].astype(F32)], axis=1)
    own[...] = jnp.concatenate([mine, jnp.zeros((8, GROUP + WIDE), F32)], axis=0).astype(BF)
    send(own, other, PAIR, pair_dev)

    def attend_one(w):
        def unit(h, carry):
            def lanes(part):
                return pl.ds(pl.multiple_of(part * GROUP + h * HDIM, HDIM), HDIM)

            out = softmax_attend(qw[w, :, lanes(0)], qw[w, :, lanes(1)], qw[w, :, lanes(2)])
            l1f[:, pl.ds(w * 8, 8), lanes(0)] = out.reshape(16, 8, HDIM)
            return carry

        lax.fori_loop(0, 3, unit, 0)

    attend_one(0)
    arrive(other, PAIR, pair_dev)
    theirs = other[...].astype(F32)[:24]
    pair = jnp.concatenate(
        [jnp.where(xl == 0, mine, theirs), jnp.where(xl == 0, theirs, mine)], axis=0
    ).astype(BF)
    here = s0 * 8 + p0
    ga[here] = pair[:, :GROUP]
    gb[here] = pair[:, GROUP:]
    bufs = (ga, gb)

    def first_send(a, d, hop):
        slot = bufs[a].at[s0 * 8 + (p0 + (1 - 2 * d) * (1 - hop) + 8) % 8]
        send(slot, slot, FIRST[a] + d * 4 + hop - 1, first(1 - 2 * d))

    def first_step(a, hop):
        for d in range(2):
            if hop == 4 and d != a:
                continue
            slot = bufs[a].at[s0 * 8 + (p0 - (1 - 2 * d) * hop + 8) % 8]
            arrive(slot, FIRST[a] + d * 4 + hop - 1, first(2 * d - 1))
            if hop < 3 or (hop == 3 and d == a):
                first_send(a, d, hop + 1)

    def second_slot(a, s, q):
        return bufs[a].at[pl.ds(pl.multiple_of(s * 8 + q * 4, 4), 4)]

    def second_send(a, d, hop, q):
        slot = second_slot(a, (s0 + (1 - 2 * d) * (1 - hop) + 8) % 8, q)
        send(slot, slot, SECOND[a] + d * 8 + (hop - 1) * 2 + q, second(1 - 2 * d))

    def second_start(a):
        for q in range(2):
            for d in range(2):
                second_send(a, d, 1, q)

    def second_step(a, hop, q):
        for d in range(2):
            if hop == 4 and d != q:
                continue
            slot = second_slot(a, (s0 - (1 - 2 * d) * hop + 8) % 8, q)
            arrive(slot, SECOND[a] + d * 8 + (hop - 1) * 2 + q, second(2 * d - 1))
            if hop < 3 or (hop == 3 and d == q):
                second_send(a, d, hop + 1, q)

    outs = (w1, w2)
    m0, odd = s0 // 2, s0 % 2
    ready = (m0, (m0 + 3 + 2 * odd) % 4, (m0 + 1 + 2 * odd) % 4, (m0 + 2) % 4)

    def natural(a, hop):
        m = ready[hop - 1]
        src, dst = bufs[a], outs[a]

        def body(i, carry):
            one = 16 * m + (1 - c) * 2 * i + c * i
            two = one + 1 + 7 * c
            at = (1 - c) * (8 * m + i) + c * (4 * i + m)
            g0, g1 = src[one].astype(F32), src[two].astype(F32)
            rows = pl.ds(pl.multiple_of((at % 16) * 48, 48), 48)
            dst[at // 16, rows] = jnp.concatenate([g0[:24], g1[:24]], axis=0).astype(BF)
            dst[2 + at // 16, rows] = jnp.concatenate([g0[24:], g1[24:]], axis=0).astype(BF)
            return carry

        lax.fori_loop(0, 8, body, 0)

    for a in range(2):
        for d in range(2):
            first_send(a, d, 1)
    attend_one(1)
    first_step(0, 1)
    first_step(1, 1)
    attend_one(2)
    l1[...] = l1f[...].reshape(TOKENS, GROUP).astype(BF)
    for hop in range(2, 4):
        first_step(0, hop)
        first_step(1, hop)
    first_step(0, 4)
    second_start(0)
    first_step(1, 4)
    for hop in range(1, 4):
        for q in range(2):
            second_step(0, hop, q)
        if hop == 3:
            second_start(1)
        natural(0, hop)
    for q in range(2):
        second_step(0, 4, q)
    natural(0, 4)

    def partial(share, rows, n):
        return lax.dot_general(
            l1[rows], w1[share, n * 256 : (n + 1) * 256], (((1,), (1,)), ((), ())),
            preferred_element_type=F32,
        )

    everything = slice(0, TOKENS)
    for i, far in enumerate((1 - xh, xh)):
        for n in range(3):
            ps[i, :, n * 256 : (n + 1) * 256] = partial(far * 2 + 1 - c, everything, n).astype(BF)
        send(ps.at[i], pr.at[i], CORE_PART + i, core_dev)
    arrive(pr.at[0], CORE_PART, core_dev)
    for k in range(CHUNKS):
        rows = slice(k * PART, (k + 1) * PART)
        for n in range(3):
            cols = slice(n * 256, (n + 1) * 256)
            both = partial((1 - xh) * 2 + c, rows, n) + pr[0, rows, cols].astype(F32)
            qs[rows, cols] = both.astype(BF)
        send(qs.at[pl.ds(k * PART, PART)], xr.at[pl.ds(k * PART, PART)], SUM_X + k, x_dev)
    stream_in.wait()
    arrive(pr.at[1], CORE_PART + 1, core_dev)
    for n in range(3):
        cols = slice(n * 256, (n + 1) * 256)
        xf[:, cols] = partial(head, everything, n) + pr[1, :, cols].astype(F32) + st[:, cols].astype(F32)

    def take_sum(k):
        rows = pl.ds(k * PART, PART)
        arrive(xr.at[rows], SUM_X + k, x_dev)
        ub[head, rows] = (xf[rows] + xr[rows].astype(F32)).astype(BF)
        send(ub.at[head, rows], ub.at[head, rows], SHARE_X + k, x_dev)
        send(ub.at[head, rows], ub.at[head, rows], SHARE_CORE + k, core_dev)

    far_head = (head + 2) % 4
    near_head = xh * 2 + 1 - c
    last_head = (near_head + 2) % 4

    def relay(k):
        rows = pl.ds(k * PART, PART)
        arrive(ub.at[far_head, rows], SHARE_X + k, x_dev)
        send(ub.at[far_head, rows], ub.at[far_head, rows], RELAY + k, core_dev)

    def norm(k):
        rows = pl.ds(k * PART, PART)
        arrive(ub.at[near_head, rows], SHARE_CORE + k, core_dev)
        arrive(ub.at[last_head, rows], RELAY + k, core_dev)

        def body(i, carry):
            r = pl.ds(pl.multiple_of(k * PART + i * 16, 16), 16)
            values = [ub[j, r].astype(F32) for j in range(4)]
            total = sum(jnp.sum(v * v, axis=-1, keepdims=True) for v in values)
            scale = lax.rsqrt(total / (4 * SHARE) + EPSILON)
            for j in range(4):
                nb[j, r] = (values[j] * scale * gain[j]).astype(BF)
            return carry

        lax.fori_loop(0, PART // 16, body, 0)

    second_step(1, 1, 0)
    second_step(1, 1, 1)
    natural(1, 1)
    take_sum(0)
    second_step(1, 2, 0)
    take_sum(1)
    upd = pltpu.make_async_copy(ub.at[head], upd_out, lsem.at[1])
    upd.start()
    second_step(1, 2, 1)
    natural(1, 2)
    relay(0)
    second_step(1, 3, 0)
    relay(1)
    second_step(1, 3, 1)
    natural(1, 3)
    norm(0)
    norm(1)
    second_step(1, 4, 0)
    second_step(1, 4, 1)
    natural(1, 4)

    for n in range(3):
        cols = slice(n * GROUP, (n + 1) * GROUP)
        acc[:, cols] = jnp.dot(nb[0], w2[0, :, cols], preferred_element_type=F32)

        def add(j, carry):
            acc[:, cols] += jnp.dot(nb[j], w2[j, :, cols], preferred_element_type=F32)
            return carry

        lax.fori_loop(1, 4, add, 0)
    for fh in range(2):
        for f in range(2):
            for rh in range(2):
                at = ((fh * 2 + f) * 2 + rh) * 48
                pj[fh, f, rh] = acc[at : at + 48].astype(BF)

    quarters = ((1, 0), (0, 1), (0, 0))
    for i, (fh, rh) in enumerate(quarters):
        send(pj.at[fh, :, rh], hq.at[i], HALO + i, halo_to[i])

    def place(value, fh, rh):
        for f in range(2):
            at = (fh * 2 + f) * 4 + rh * 2
            x2[at : at + 2] = value[f].astype(F32).reshape(2, 24, WIDE)

    place(pj[1, :, 1], 0, 0)
    for i, (fh, rh) in enumerate(quarters):
        arrive(hq.at[i], HALO + i, halo_from[i])
        place(hq[i], 1 - fh, 1 - rh)

    for w in range(3):
        for h in range(3):
            def window(part):
                lanes = slice(part * GROUP + h * HDIM, part * GROUP + (h + 1) * HDIM)
                return x2[:, w * 8 : w * 8 + 8, lanes].reshape(128, HDIM).astype(BF)

            out = softmax_attend(window(0), window(1), window(2))
            o2[:, w * 8 : w * 8 + 8, h * HDIM : (h + 1) * HDIM] = out.reshape(16, 8, HDIM)

    def result(fh, f, rh):
        at = (fh * 2 + f) * 4 + rh * 2
        return o2[at : at + 2].reshape(48, GROUP).astype(BF)

    for i, (fh, rh) in enumerate(quarters):
        for f in range(2):
            ob[1 - fh, f, 1 - rh] = result(1 - fh, f, 1 - rh)
        send(ob.at[1 - fh, :, 1 - rh], lb.at[fh, :, rh], BACK + i, halo_from[i])
    for f in range(2):
        lb[1, f, 1] = result(0, f, 0)
    for i, (fh, rh) in enumerate(quarters):
        arrive(lb.at[fh, :, rh], BACK + i, halo_to[i])
    two = pltpu.make_async_copy(lb, two_out, lsem.at[2])
    two.start()
    for copy in sent:
        copy.wait_send()
    upd.wait()
    two.wait()


def shards(stream, qkv1, w_out1, gain, w_qkv2):
    frames, tile_rows, tile_cols, channels = stream.shape
    windowed = qkv1.reshape(16, 3, 8, WIDE).transpose(1, 0, 2, 3).reshape(3, 128, WIDE)
    vmem = pl.BlockSpec(memory_space=pltpu.VMEM)
    anywhere = pl.BlockSpec(memory_space=pl.ANY)
    updated, layer_two = pl.pallas_call(
        kernel,
        name="layers",
        out_shape=(
            jax.ShapeDtypeStruct((TOKENS, SHARE), BF),
            jax.ShapeDtypeStruct((2, 2, 2, 48, GROUP), BF),
        ),
        in_specs=[vmem, vmem, vmem, vmem, anywhere],
        out_specs=(anywhere, anywhere),
        scratch_shapes=[
            pltpu.VMEM((32, GROUP + WIDE), BF),
            pltpu.VMEM((32, GROUP + WIDE), BF),
            pltpu.VMEM((64, 48, GROUP), BF),
            pltpu.VMEM((64, 48, WIDE), BF),
            pltpu.VMEM((4, SHARE, GROUP), BF),
            pltpu.VMEM((4, SHARE, WIDE), BF),
            pltpu.VMEM((16, 24, GROUP), F32),
            pltpu.VMEM((TOKENS, GROUP), BF),
            pltpu.VMEM((2, TOKENS, SHARE), BF),
            pltpu.VMEM((2, TOKENS, SHARE), BF),
            pltpu.VMEM((TOKENS, SHARE), BF),
            pltpu.VMEM((TOKENS, SHARE), BF),
            pltpu.VMEM((TOKENS, SHARE), F32),
            pltpu.VMEM((TOKENS, SHARE), BF),
            pltpu.VMEM((4, TOKENS, SHARE), BF),
            pltpu.VMEM((4, TOKENS, SHARE), BF),
            pltpu.VMEM((TOKENS, WIDE), F32),
            pltpu.VMEM((2, 2, 2, 48, WIDE), BF),
            pltpu.VMEM((3, 2, 48, WIDE), BF),
            pltpu.VMEM((16, 24, WIDE), F32),
            pltpu.VMEM((16, 24, GROUP), F32),
            pltpu.VMEM((2, 2, 2, 48, GROUP), BF),
            pltpu.VMEM((2, 2, 2, 48, GROUP), BF),
            pltpu.SemaphoreType.DMA((N_SEM,)),
            pltpu.SemaphoreType.DMA((N_SEM,)),
            pltpu.SemaphoreType.DMA((3,)),
        ],
        compiler_params=pltpu.CompilerParams(
            collective_id=0, has_side_effects=True, vmem_limit_bytes=56 * 2**20
        ),
    )(
        windowed,
        w_out1,
        w_qkv2.reshape(24, WIDE),
        gain.reshape(4, 1, SHARE),
        stream.reshape(TOKENS, channels),
    )
    return (
        updated.reshape(frames, tile_rows, tile_cols, SHARE),
        layer_two.reshape(frames, tile_rows, tile_cols, GROUP),
    )


def solution(mesh):
    in_specs = (
        P("tm", "row", None, None),
        P("tm", "row", None, None, "head"),
        P(("row", "tm"), "head"),
        P(),
        P(("row", "tm"), None, "head"),
    )
    out_specs = (P("tm", "row", None, "head"), P("tm", "row", None, "head"))
    return jax.shard_map(shards, mesh=mesh, in_specs=in_specs, out_specs=out_specs, check_vma=False)
```

time: 1350 us -> 127 us (0.09)
  the two profiles are of different devices: /device:TPU:4 before, /device:TPU:1 now
where the time goes in v1:
time: 127 us
  Pallas kernels  118 us (93%)
  local copies, waits for them, and re-layouts  7.71 us (6%)
    pallas_call x1, Pallas kernels, shards(): pl.pallas_call(kernel, name='layers', out_shape=(jax.ShapeDtypeStruct((TO...  118 us
    unnamed x5, local copies, waits for them, and re-layouts  5.29 us

profile of v1, /device:TPU:1, one launch (start us, length us, event | category | flops | bytes accessed | tf_op | source)
XLA Modules:
  0.0 126.5 jit_solution(13927765908564206626)
XLA Ops:
  0.6 1.7 %copy.8 = bf16[4,4,24,3,384]{4,3,2,1,0:T(4,128)(2,1)S(1)} copy(bf16[4,4,24,3,384]{4,2,3,1,0:T(8,128)(2,1)} %param.6) | data formatting | bytes 1769472 | tf_op args[1]
  2.3 0.0 copy-start
  2.3 0.8 reshape.25
  3.1 1.0 copy_bitcast_fusion.qw
  4.1 0.0 copy-done
  4.1 0.6 copy.11
  4.7 118.2 %layers.1 = (bf16[384,768]{1,0:T(8,128)(2,1)}, bf16[2,2,2,48,384]{4,3,2,1,0:T(8,128)(2,1)}) custom-call(bf16[3,128,1152]{2,1,0:T(8,128)(2,1)} %copy_bitcast_fusion.qw, bf16[24,384]{1,0:T(8,128)(2,1)} %wo.1, bf16[24,1152]{1,0:T(8,128)(2,1)} %bitcast.14, f32[4,1,768]{2,1,0:T(1,128)} %bitcast.16, bf16[384,3072]{1,0:T(8,128)(2,1)} %bitcast.11), custom_call_target="tpu_custom_call" | custom-call | tf_op jit(solution)/shard_map/layers/pallas_call | solution.py:342
  122.9 1.9 %copy.15 = bf16[4,4,24,768]{3,2,1,0:T(8,128)(2,1)} copy(bf16[4,4,24,768]{3,2,1,0:T(8,128)(2,1)} %bitcast.12) | data formatting | bytes 1179648
  124.8 1.7 %copy.16 = bf16[4,4,24,384]{3,2,1,0:T(8,128)(2,1)} copy(bf16[4,4,24,384]{3,2,1,0:T(8,128)(2,1)} %bitcast.13) | data formatting | bytes 589824
Async XLA Ops:
  2.3 1.8 %copy-start = (bf16[24,3,384]{2,0,1:T(8,128)(2,1)S(1)}, bf16[24,3,384]{2,0,1:T(8,128)(2,1)}, u32[]{:S(2)}) copy-start(bf16[24,3,384]{2,0,1:T(8,128)(2,1)} %param.9) | copy-start | bytes 165892

commit v2 on v1

v2 whole, which is shorter than its diff:
```python
import jax
import jax.numpy as jnp
from jax import lax
from jax.experimental import pallas as pl
from jax.experimental.pallas import tpu as pltpu
from jax.sharding import PartitionSpec as P

MESH = pl.DeviceIdType.MESH
HDIM = 128
EPSILON = 1e-06
TOKENS = 384
SHARE = 768
GROUP = 384
WIDE = 1152
CHUNKS = 2
PART = TOKENS // CHUNKS
BF = jnp.bfloat16
F32 = jnp.float32

FIRST = (0, 8)
SECOND = (16, 32)
PAIR = 48
LINE = 49
LAYER_ONE = 52
CORE_PART = 53
SHARE_X = 54
SHARE_CORE = SHARE_X + CHUNKS
RELAY = SHARE_CORE + CHUNKS
HALO = RELAY + CHUNKS
BACK = HALO + 9
N_SEM = BACK + 9


def softmax_attend(q, k, v):
    scores = lax.dot_general(
        q, k, (((1,), (1,)), ((), ())), preferred_element_type=F32
    ) * HDIM ** (-0.5)
    largest = jnp.max(scores, axis=-1, keepdims=True)
    weights = jnp.exp(scores - largest)
    probabilities = (weights / jnp.sum(weights, axis=-1, keepdims=True)).astype(BF)
    return jnp.dot(probabilities, v, preferred_element_type=F32)


def kernel(
    qkv, wo, wq, gain, stream, upd_out, two_out,
    own, other, line, ga, gb, w1, w2, x1, l1f, l1, ps, pr, xf, st, ub, nb, pj, hq, x2, o2, ob, lb,
    ssem, rsem, lsem,
):
    row = lax.axis_index("row")
    z = lax.axis_index("tm")
    head = lax.axis_index("head")
    xl, y = row // 8, row % 8
    xh, c = head // 2, head % 2

    def first(d):
        return (xl * 8 + (y + c * (d + 8)) % 8, (z + (1 - c) * (d + 8)) % 8, head)

    def second(d):
        return (xl * 8 + (y + (1 - c) * (d + 8)) % 8, (z + c * (d + 8)) % 8, head)

    p0 = (1 - c) * z + c * y
    s0 = (1 - c) * y + c * z
    pair_dev = ((row + 8) % 16, z, head)
    core_dev = (row, z, xh * 2 + (1 - c))
    x_dev = (row, z, (head + 2) % 4)
    cross_dev = ((row + 8) % 16, z, (head + 2) % 4)
    row_m, row_p = (row + 15) % 16, (row + 1) % 16
    z_m, z_p = (z + 7) % 8, (z + 1) % 8
    lower = ((row_m, z, head), (row, z_m, head), (row_m, z_m, head))
    upper = ((row_p, z, head), (row, z_p, head), (row_p, z_p, head))

    barrier = pltpu.get_barrier_semaphore()
    greet = (first(1), first(-1), second(1), second(-1), pair_dev, core_dev, x_dev, cross_dev) + lower + upper
    for device in greet:
        pl.semaphore_signal(barrier, inc=1, device_id=device, device_id_type=MESH)
    pl.semaphore_wait(barrier, len(greet))

    sent = []

    def send(src, dst, k, device):
        copy = pltpu.make_async_remote_copy(
            src_ref=src, dst_ref=dst, send_sem=ssem.at[k], recv_sem=rsem.at[k],
            device_id=device, device_id_type=MESH,
        )
        copy.start()
        sent.append(copy)

    def arrive(dst, k, device):
        pltpu.make_async_remote_copy(
            src_ref=dst, dst_ref=dst, send_sem=ssem.at[k], recv_sem=rsem.at[k],
            device_id=device, device_id_type=MESH,
        ).wait_recv()

    at_x = xh * 2 + xl
    tail = jnp.zeros((8, GROUP), F32)
    line[at_x] = jnp.concatenate([wo[...].astype(F32), tail], axis=0).astype(BF)
    for i, device in enumerate((pair_dev, x_dev, cross_dev)):
        send(line.at[at_x], line.at[at_x], LINE + i, device)
    mine = jnp.concatenate(
        [wq[part, :, h * HDIM : (h + 1) * HDIM].astype(F32) for h in range(3) for part in range(3)], axis=1
    )
    own[...] = jnp.concatenate([mine, jnp.zeros((8, WIDE), F32)], axis=0).astype(BF)
    send(own, other, PAIR, pair_dev)

    stream_in = pltpu.make_async_copy(
        stream.at[:, pl.ds(pl.multiple_of(head * SHARE, SHARE), SHARE)], st, lsem.at[0]
    )
    stream_in.start()

    def widen(i, carry):
        for part in range(3):
            x1[part, i] = qkv[i, part].astype(F32)
        return carry

    lax.fori_loop(0, 16, widen, 0)

    def attend_one(w):
        def unit(h, carry):
            lanes = pl.ds(pl.multiple_of(h * HDIM, HDIM), HDIM)

            def window(part):
                return x1[part, :, w * 8 : w * 8 + 8, lanes].reshape(128, HDIM).astype(BF)

            out = softmax_attend(window(0), window(1), window(2))
            l1f[:, w * 8 : w * 8 + 8, lanes] = out.reshape(16, 8, HDIM)
            return carry

        lax.fori_loop(0, 3, unit, 0)

    def at_line(flip_low, flip_high):
        return (xh + flip_high * (1 - 2 * xh)) * 2 + xl + flip_low * (1 - 2 * xl)

    arrive(line.at[at_line(1, 0)], LINE, pair_dev)
    arrive(line.at[at_line(0, 1)], LINE + 1, x_dev)
    arrive(line.at[at_line(1, 1)], LINE + 2, cross_dev)
    here = s0 * 8 + p0
    ga[here] = jnp.concatenate(
        [line[xh].astype(F32)[:24], line[2 + xh].astype(F32)[:24]], axis=0
    ).astype(BF)
    bufs = (ga, gb)

    def first_send(a, d, hop):
        slot = bufs[a].at[s0 * 8 + (p0 + (1 - 2 * d) * (1 - hop) + 8) % 8]
        send(slot, slot, FIRST[a] + d * 4 + hop - 1, first(1 - 2 * d))

    def first_step(a, hop):
        for d in range(2):
            if hop == 4 and d != a:
                continue
            slot = bufs[a].at[s0 * 8 + (p0 - (1 - 2 * d) * hop + 8) % 8]
            arrive(slot, FIRST[a] + d * 4 + hop - 1, first(2 * d - 1))
            if hop < 3 or (hop == 3 and d == a):
                first_send(a, d, hop + 1)

    def second_slot(a, s, q):
        return bufs[a].at[pl.ds(pl.multiple_of(s * 8 + q * 4, 4), 4)]

    def second_send(a, d, hop, q):
        slot = second_slot(a, (s0 + (1 - 2 * d) * (1 - hop) + 8) % 8, q)
        send(slot, slot, SECOND[a] + d * 8 + (hop - 1) * 2 + q, second(1 - 2 * d))

    def second_start(a, q):
        for d in range(2):
            second_send(a, d, 1, q)

    def second_step(a, hop, q):
        for d in range(2):
            if hop == 4 and d != q:
                continue
            slot = second_slot(a, (s0 - (1 - 2 * d) * hop + 8) % 8, q)
            arrive(slot, SECOND[a] + d * 8 + (hop - 1) * 2 + q, second(2 * d - 1))
            if hop < 3 or (hop == 3 and d == q):
                second_send(a, d, hop + 1, q)

    outs = (w1, w2)
    m0, odd = s0 // 2, s0 % 2
    ready = (m0, (m0 + 3 + 2 * odd) % 4, (m0 + 1 + 2 * odd) % 4, (m0 + 2) % 4)

    def natural(a, hop):
        m = ready[hop - 1]
        src, dst = bufs[a], outs[a]

        def body(i, carry):
            one = 16 * m + (1 - c) * 2 * i + c * i
            two = one + 1 + 7 * c
            at = (1 - c) * (8 * m + i) + c * (4 * i + m)
            g0, g1 = src[one].astype(F32), src[two].astype(F32)
            rows = pl.ds(pl.multiple_of(at * 48, 48), 48)
            dst[0, rows] = jnp.concatenate([g0[:24], g1[:24]], axis=0).astype(BF)
            dst[1, rows] = jnp.concatenate([g0[24:], g1[24:]], axis=0).astype(BF)
            return carry

        lax.fori_loop(0, 8, body, 0)

    for d in range(2):
        first_send(0, d, 1)
    arrive(other, PAIR, pair_dev)
    theirs = other[...].astype(F32)[:24]
    gb[here] = jnp.concatenate(
        [jnp.where(xl == 0, mine, theirs), jnp.where(xl == 0, theirs, mine)], axis=0
    ).astype(BF)
    for d in range(2):
        first_send(1, d, 1)
    attend_one(0)
    first_step(0, 1)
    first_step(1, 1)
    attend_one(1)
    first_step(0, 2)
    first_step(1, 2)
    attend_one(2)
    first_step(0, 3)
    first_step(1, 3)
    l1[xh] = l1f[...].reshape(TOKENS, GROUP).astype(BF)
    send(l1.at[xh], l1.at[xh], LAYER_ONE, x_dev)
    first_step(0, 4)
    second_start(0, 0)
    second_start(0, 1)
    first_step(1, 4)
    second_start(1, 0)
    second_step(0, 1, 0)
    second_step(0, 1, 1)
    second_start(1, 1)
    second_step(0, 2, 0)
    second_step(0, 2, 1)
    natural(0, 1)
    second_step(1, 1, 0)
    second_step(0, 3, 0)
    second_step(0, 3, 1)
    natural(0, 2)
    second_step(1, 1, 1)
    natural(0, 3)
    second_step(0, 4, 0)
    second_step(0, 4, 1)
    natural(0, 4)

    arrive(l1.at[1 - xh], LAYER_ONE, x_dev)

    def partial(share, n):
        rows = pl.ds(pl.multiple_of(share * SHARE + n * 256, 256), 256)
        return sum(
            lax.dot_general(
                l1[j], w1[j, rows], (((1,), (1,)), ((), ())), preferred_element_type=F32
            )
            for j in range(2)
        )

    for n in range(3):
        ps[:, n * 256 : (n + 1) * 256] = partial(1 - c, n).astype(BF)
    send(ps, pr, CORE_PART, core_dev)
    stream_in.wait()
    for n in range(3):
        cols = slice(n * 256, (n + 1) * 256)
        xf[:, cols] = partial(c, n) + st[:, cols].astype(F32)
    arrive(pr, CORE_PART, core_dev)
    for k in range(CHUNKS):
        rows = pl.ds(k * PART, PART)
        ub[head, rows] = (xf[rows] + pr[rows].astype(F32)).astype(BF)
        send(ub.at[head, rows], ub.at[head, rows], SHARE_X + k, x_dev)
        send(ub.at[head, rows], ub.at[head, rows], SHARE_CORE + k, core_dev)
    upd = pltpu.make_async_copy(ub.at[head], upd_out, lsem.at[1])
    upd.start()

    far_head = (head + 2) % 4
    near_head = xh * 2 + 1 - c
    last_head = (near_head + 2) % 4

    def relay(k):
        rows = pl.ds(k * PART, PART)
        arrive(ub.at[far_head, rows], SHARE_X + k, x_dev)
        send(ub.at[far_head, rows], ub.at[far_head, rows], RELAY + k, core_dev)

    def norm(k):
        rows = pl.ds(k * PART, PART)
        arrive(ub.at[near_head, rows], SHARE_CORE + k, core_dev)
        arrive(ub.at[last_head, rows], RELAY + k, core_dev)

        def body(i, carry):
            r = pl.ds(pl.multiple_of(k * PART + i * 16, 16), 16)
            values = [ub[j, r].astype(F32) for j in range(4)]
            total = sum(jnp.sum(v * v, axis=-1, keepdims=True) for v in values)
            scale = lax.rsqrt(total / (4 * SHARE) + EPSILON)
            for j in range(4):
                nb[r, j * SHARE : (j + 1) * SHARE] = (values[j] * scale * gain[j]).astype(BF)
            return carry

        lax.fori_loop(0, PART // 16, body, 0)

    second_step(1, 2, 0)
    natural(1, 1)
    second_step(1, 2, 1)
    natural(1, 2)
    relay(0)
    second_step(1, 3, 0)
    relay(1)
    norm(0)
    second_step(1, 3, 1)
    natural(1, 3)
    norm(1)
    second_step(1, 4, 0)
    second_step(1, 4, 1)
    natural(1, 4)

    order = (0, 2, 1)
    sides = {0: 1, 1: 1, 2: 0}

    def quarters(a):
        return ((a, 1 - a), (1 - a, a), (1 - a, 1 - a))

    for h in order:
        a = sides[h]
        to = lower if a else upper
        lanes = slice(h * GROUP, (h + 1) * GROUP)
        whole = sum(
            jnp.dot(nb[:, j * 1536 : (j + 1) * 1536], w2[j, :, lanes], preferred_element_type=F32)
            for j in range(2)
        )
        for fh in range(2):
            for f in range(2):
                for rh in range(2):
                    at = ((fh * 2 + f) * 2 + rh) * 48
                    pj[h, fh, f, rh] = whole[at : at + 48].astype(BF)
        for i, (fh, rh) in enumerate(quarters(a)):
            send(pj.at[h, fh, :, rh], hq.at[h, i], HALO + h * 3 + i, to[i])

    for h in order:
        a = sides[h]
        source = upper if a else lower

        def place(value, fh, rh):
            for f in range(2):
                at = (fh * 2 + f) * 4 + rh * 2
                x2[h, at : at + 2] = value[f].astype(F32).reshape(2, 24, GROUP)

        place(pj[h, a, :, a], 1 - a, 1 - a)
        for i, (fh, rh) in enumerate(quarters(a)):
            arrive(hq.at[h, i], HALO + h * 3 + i, source[i])
            place(hq[h, i], 1 - fh, 1 - rh)
        for w in range(3):
            def window(part):
                return x2[h, :, w * 8 : w * 8 + 8, part * HDIM : (part + 1) * HDIM].reshape(128, HDIM).astype(BF)

            out = softmax_attend(window(0), window(1), window(2))
            o2[h, :, w * 8 : w * 8 + 8] = out.reshape(16, 8, HDIM)

        def result(fh, f, rh):
            at = (fh * 2 + f) * 4 + rh * 2
            return o2[h, at : at + 2].reshape(48, HDIM).astype(BF)

        lanes = pl.ds(h * HDIM, HDIM)
        for i, (fh, rh) in enumerate(quarters(a)):
            for f in range(2):
                ob[h, fh, f, rh] = result(1 - fh, f, 1 - rh)
            send(ob.at[h, fh, :, rh], lb.at[fh, :, rh, :, lanes], BACK + h * 3 + i, source[i])
        for f in range(2):
            lb[a, f, a, :, lanes] = result(1 - a, f, 1 - a)
    for h in order:
        a = sides[h]
        to = lower if a else upper
        for i, (fh, rh) in enumerate(quarters(a)):
            arrive(lb.at[fh, :, rh, :, pl.ds(h * HDIM, HDIM)], BACK + h * 3 + i, to[i])
    two = pltpu.make_async_copy(lb, two_out, lsem.at[2])
    two.start()
    for copy in sent:
        copy.wait_send()
    upd.wait()
    two.wait()


def shards(stream, qkv1, w_out1, gain, w_qkv2):
    frames, tile_rows, tile_cols, channels = stream.shape
    vmem = pl.BlockSpec(memory_space=pltpu.VMEM)
    anywhere = pl.BlockSpec(memory_space=pl.ANY)
    updated, layer_two = pl.pallas_call(
        kernel,
        name="layers",
        out_shape=(
            jax.ShapeDtypeStruct((TOKENS, SHARE), BF),
            jax.ShapeDtypeStruct((2, 2, 2, 48, GROUP), BF),
        ),
        in_specs=[vmem, vmem, vmem, vmem, anywhere],
        out_specs=(anywhere, anywhere),
        scratch_shapes=[
            pltpu.VMEM((32, WIDE), BF),
            pltpu.VMEM((32, WIDE), BF),
            pltpu.VMEM((4, 32, GROUP), BF),
            pltpu.VMEM((64, 48, GROUP), BF),
            pltpu.VMEM((64, 48, WIDE), BF),
            pltpu.VMEM((2, 1536, GROUP), BF),
            pltpu.VMEM((2, 1536, WIDE), BF),
            pltpu.VMEM((3, 16, 24, GROUP), F32),
            pltpu.VMEM((16, 24, GROUP), F32),
            pltpu.VMEM((2, TOKENS, GROUP), BF),
            pltpu.VMEM((TOKENS, SHARE), BF),
            pltpu.VMEM((TOKENS, SHARE), BF),
            pltpu.VMEM((TOKENS, SHARE), F32),
            pltpu.VMEM((TOKENS, SHARE), BF),
            pltpu.VMEM((4, TOKENS, SHARE), BF),
            pltpu.VMEM((TOKENS, 4 * SHARE), BF),
            pltpu.VMEM((3, 2, 2, 2, 48, GROUP), BF),
            pltpu.VMEM((3, 3, 2, 48, GROUP), BF),
            pltpu.VMEM((3, 16, 24, GROUP), F32),
            pltpu.VMEM((3, 16, 24, HDIM), F32),
            pltpu.VMEM((3, 2, 2, 2, 48, HDIM), BF),
            pltpu.VMEM((2, 2, 2, 48, GROUP), BF),
            pltpu.SemaphoreType.DMA((N_SEM,)),
            pltpu.SemaphoreType.DMA((N_SEM,)),
            pltpu.SemaphoreType.DMA((3,)),
        ],
        compiler_params=pltpu.CompilerParams(
            collective_id=0, has_side_effects=True, vmem_limit_bytes=56 * 2**20
        ),
    )(
        qkv1.transpose(0, 1, 3, 2, 4).reshape(16, 3, 24, GROUP),
        w_out1,
        w_qkv2.transpose(1, 0, 2),
        gain.reshape(4, 1, SHARE),
        stream.reshape(TOKENS, channels),
    )
    return (
        updated.reshape(frames, tile_rows, tile_cols, SHARE),
        layer_two.reshape(frames, tile_rows, tile_cols, GROUP),
    )


def solution(mesh):
    in_specs = (
        P("tm", "row", None, None),
        P("tm", "row", None, None, "head"),
        P(("row", "tm"), "head"),
        P(),
        P(("row", "tm"), None, "head"),
    )
    out_specs = (P("tm", "row", None, "head"), P("tm", "row", None, "head"))
    return jax.shard_map(shards, mesh=mesh, in_specs=in_specs, out_specs=out_specs, check_vma=False)
```

time: 127 us -> 114 us (0.90)
  Pallas kernels: 118 us -> 108 us
  local copies, waits for them, and re-layouts: 7.71 us -> 3.62 us
    pallas_call x1, Pallas kernels: 118 us -> 108 us  [shards(): pl.pallas_call(kernel, name='layers', out_shape=(jax.ShapeDtypeStruct((TO...]
    reshape x3 -> x0, local copies, waits for them, and re-layouts: 2.42 us -> none  [the longest x2 1.79 us: shards(): qkv1.reshape(16, 3, 8, WIDE).transpose(1, 0, 2, 3).reshape(3, 128, WIDE)]
    unnamed x5 -> x2, local copies, waits for them, and re-layouts: 5.29 us -> 3.62 us
where the time goes in v2:
time: 114 us; the launch traced here: 113 us
  Pallas kernels  108 us (95%)
  local copies, waits for them, and re-layouts  3.62 us (3%)
    pallas_call x1, Pallas kernels, shards(): pl.pallas_call(kernel, name='layers', out_shape=(jax.ShapeDtypeStruct((TO...  108 us
    unnamed x2, local copies, waits for them, and re-layouts  3.62 us

profile of v2, /device:TPU:1, one launch (start us, length us, event | category | flops | bytes accessed | tf_op | source)
XLA Modules:
  0.0 112.7 jit_solution(8810434654429753907)
XLA Ops:
  0.6 108.5 %layers.1 = (bf16[384,768]{1,0:T(8,128)(2,1)}, bf16[2,2,2,48,384]{4,3,2,1,0:T(8,128)(2,1)}) custom-call(bf16[16,3,24,384]{3,2,1,0:T(8,128)(2,1)} %bitcast.9, bf16[24,384]{1,0:T(8,128)(2,1)} %wo.1, bf16[3,24,384]{2,1,0:T(8,128)(2,1)} %bitcast.12, f32[4,1,768]{2,1,0:T(1,128)} %bitcast.13, bf16[384,3072]{1,0:T(8,128)(2,1)} %bitcast.8), custom_call_target="tpu_custom_call" | custom-call | tf_op jit(solution)/shard_map/layers/pallas_call | solution.py:373
  109.1 1.9 %copy.9 = bf16[4,4,24,768]{3,2,1,0:T(8,128)(2,1)} copy(bf16[4,4,24,768]{3,2,1,0:T(8,128)(2,1)} %bitcast.10) | data formatting | bytes 1179648
  111.0 1.7 %copy.10 = bf16[4,4,24,384]{3,2,1,0:T(8,128)(2,1)} copy(bf16[4,4,24,384]{3,2,1,0:T(8,128)(2,1)} %bitcast.11) | data formatting | bytes 589824

commit v3 on v2

--- a/solution.py
+++ b/solution.py
@@ -17,13 +17,17 @@
 BF = jnp.bfloat16
 F32 = jnp.float32
 
+OFFSETS = (1, -1, 2, -2, 3, -3, 4)
+
+GROUPS = ((0,), (1, -1), (2, -2), (3, -3), (4,))
+
 FIRST = (0, 8)
 SECOND = (16, 32)
-PAIR = 48
-LINE = 49
-LAYER_ONE = 52
-CORE_PART = 53
-SHARE_X = 54
+PAIR = 96
+LINE = 97
+LAYER_ONE = 100
+CORE_PART = 101
+SHARE_X = 102
 SHARE_CORE = SHARE_X + CHUNKS
 RELAY = SHARE_CORE + CHUNKS
 HALO = RELAY + CHUNKS
@@ -70,7 +74,8 @@
     upper = ((row_p, z, head), (row, z_p, head), (row_p, z_p, head))
 
     barrier = pltpu.get_barrier_semaphore()
-    greet = (first(1), first(-1), second(1), second(-1), pair_dev, core_dev, x_dev, cross_dev) + lower + upper
+    greet = (second(1), second(-1), pair_dev, core_dev, x_dev, cross_dev) + lower + upper
+    greet += tuple(first(d) for d in OFFSETS)
     for device in greet:
         pl.semaphore_signal(barrier, inc=1, device_id=device, device_id_type=MESH)
     pl.semaphore_wait(barrier, len(greet))
@@ -112,8 +117,6 @@
             x1[part, i] = qkv[i, part].astype(F32)
         return carry
 
-    lax.fori_loop(0, 16, widen, 0)
-
     def attend_one(w):
         def unit(h, carry):
             lanes = pl.ds(pl.multiple_of(h * HDIM, HDIM), HDIM)
@@ -139,38 +142,75 @@
     ).astype(BF)
     bufs = (ga, gb)
 
-    def first_send(a, d, hop):
-        slot = bufs[a].at[s0 * 8 + (p0 + (1 - 2 * d) * (1 - hop) + 8) % 8]
-        send(slot, slot, FIRST[a] + d * 4 + hop - 1, first(1 - 2 * d))
-
-    def first_step(a, hop):
+    def spread():
+        for i, d in enumerate(OFFSETS):
+            send(ga.at[here], ga.at[here], FIRST[0] + i, first(d))
+
+    def spread_arrive():
+        for i, d in enumerate(OFFSETS):
+            arrive(ga.at[s0 * 8 + (p0 - d + 8) % 8], FIRST[0] + i, first(-d))
+
+    def first_send(d, hop):
+        slot = gb.at[s0 * 8 + (p0 + (1 - 2 * d) * (1 - hop) + 8) % 8]
+        send(slot, slot, FIRST[1] + d * 4 + hop - 1, first(1 - 2 * d))
+
+    def first_step(hop):
         for d in range(2):
-            if hop == 4 and d != a:
+            if hop == 4 and d == 0:
                 continue
-            slot = bufs[a].at[s0 * 8 + (p0 - (1 - 2 * d) * hop + 8) % 8]
-            arrive(slot, FIRST[a] + d * 4 + hop - 1, first(2 * d - 1))
-            if hop < 3 or (hop == 3 and d == a):
-                first_send(a, d, hop + 1)
-
-    def second_slot(a, s, q):
-        return bufs[a].at[pl.ds(pl.multiple_of(s * 8 + q * 4, 4), 4)]
-
-    def second_send(a, d, hop, q):
-        slot = second_slot(a, (s0 + (1 - 2 * d) * (1 - hop) + 8) % 8, q)
-        send(slot, slot, SECOND[a] + d * 8 + (hop - 1) * 2 + q, second(1 - 2 * d))
-
-    def second_start(a, q):
-        for d in range(2):
-            second_send(a, d, 1, q)
-
-    def second_step(a, hop, q):
-        for d in range(2):
-            if hop == 4 and d != q:
-                continue
-            slot = second_slot(a, (s0 - (1 - 2 * d) * hop + 8) % 8, q)
-            arrive(slot, SECOND[a] + d * 8 + (hop - 1) * 2 + q, second(2 * d - 1))
-            if hop < 3 or (hop == 3 and d == q):
-                second_send(a, d, hop + 1, q)
+            slot = gb.at[s0 * 8 + (p0 - (1 - 2 * d) * hop + 8) % 8]
+            arrive(slot, FIRST[1] + d * 4 + hop - 1, first(2 * d - 1))
+            if hop < 3 or (hop == 3 and d == 1):
+                first_send(d, hop + 1)
+
+    def slab_slot(s, q):
+        return ga.at[pl.ds(pl.multiple_of(s * 8 + q * 4, 4), 4)]
+
+    def slab_send(d, hop, q):
+        slot = slab_slot((s0 + (1 - 2 * d) * (1 - hop) + 8) % 8, q)
+        send(slot, slot, SECOND[0] + d * 8 + (hop - 1) * 2 + q, second(1 - 2 * d))
+
+    def slab_start():
+        for q in range(2):
+            for d in range(2):
+                slab_send(d, 1, q)
+
+    def slab_step(hop):
+        for q in range(2):
+            for d in range(2):
+                if hop == 4 and d != q:
+                    continue
+                slot = slab_slot((s0 - (1 - 2 * d) * hop + 8) % 8, q)
+                arrive(slot, SECOND[0] + d * 8 + (hop - 1) * 2 + q, second(2 * d - 1))
+                if hop < 3 or (hop == 3 and d == q):
+                    slab_send(d, hop + 1, q)
+
+    def shard_slot(s, o):
+        return gb.at[s * 8 + (p0 + o + 8) % 8]
+
+    def shard_number(d, hop, o):
+        return SECOND[1] + (hop - 1) * 16 + (o % 8) * 2 + d
+
+    def shard_send(d, hop, o):
+        slot = shard_slot((s0 + (1 - 2 * d) * (1 - hop) + 8) % 8, o)
+        send(slot, slot, shard_number(d, hop, o), second(1 - 2 * d))
+
+    def shard_start(g):
+        for o in GROUPS[g]:
+            for d in range(2):
+                shard_send(d, 1, o)
+
+    def shard_step(hop, *groups):
+        for g in groups:
+            for o in GROUPS[g]:
+                for d in range(2):
+                    last = d == (0 if o > 0 else 1)
+                    if hop == 4 and not last:
+                        continue
+                    slot = shard_slot((s0 - (1 - 2 * d) * hop + 8) % 8, o)
+                    arrive(slot, shard_number(d, hop, o), second(2 * d - 1))
+                    if hop < 3 or (hop == 3 and last):
+                        shard_send(d, hop + 1, o)
 
     outs = (w1, w2)
     m0, odd = s0 // 2, s0 % 2
@@ -192,45 +232,41 @@
 
         lax.fori_loop(0, 8, body, 0)
 
-    for d in range(2):
-        first_send(0, d, 1)
+    spread()
     arrive(other, PAIR, pair_dev)
     theirs = other[...].astype(F32)[:24]
     gb[here] = jnp.concatenate(
         [jnp.where(xl == 0, mine, theirs), jnp.where(xl == 0, theirs, mine)], axis=0
     ).astype(BF)
     for d in range(2):
-        first_send(1, d, 1)
+        first_send(d, 1)
+    shard_start(0)
+    lax.fori_loop(0, 16, widen, 0)
     attend_one(0)
-    first_step(0, 1)
-    first_step(1, 1)
+    first_step(1)
+    shard_start(1)
+    spread_arrive()
+    slab_start()
+    first_step(2)
+    shard_start(2)
     attend_one(1)
-    first_step(0, 2)
-    first_step(1, 2)
+    first_step(3)
+    shard_start(3)
+    slab_step(1)
+    first_step(4)
+    shard_start(4)
+    shard_step(1, 0)
     attend_one(2)
-    first_step(0, 3)
-    first_step(1, 3)
     l1[xh] = l1f[...].reshape(TOKENS, GROUP).astype(BF)
     send(l1.at[xh], l1.at[xh], LAYER_ONE, x_dev)
-    first_step(0, 4)
-    second_start(0, 0)
-    second_start(0, 1)
-    first_step(1, 4)
-    second_start(1, 0)
-    second_step(0, 1, 0)
-    second_step(0, 1, 1)
-    second_start(1, 1)
-    second_step(0, 2, 0)
-    second_step(0, 2, 1)
+    slab_step(2)
     natural(0, 1)
-    second_step(1, 1, 0)
-    second_step(0, 3, 0)
-    second_step(0, 3, 1)
+    shard_step(1, 1, 2)
+    slab_step(3)
     natural(0, 2)
-    second_step(1, 1, 1)
+    shard_step(1, 3)
     natural(0, 3)
-    second_step(0, 4, 0)
-    second_step(0, 4, 1)
+    slab_step(4)
     natural(0, 4)
 
     arrive(l1.at[1 - xh], LAYER_ONE, x_dev)
@@ -285,19 +321,20 @@
 
         lax.fori_loop(0, PART // 16, body, 0)
 
-    second_step(1, 2, 0)
+    shard_step(1, 4)
+    shard_step(2, 0, 1)
     natural(1, 1)
-    second_step(1, 2, 1)
+    shard_step(2, 2, 3, 4)
+    relay(0)
     natural(1, 2)
-    relay(0)
-    second_step(1, 3, 0)
+    shard_step(3, 0, 1)
     relay(1)
     norm(0)
-    second_step(1, 3, 1)
+    shard_step(3, 2, 3)
+    norm(1)
+    shard_step(3, 4)
     natural(1, 3)
-    norm(1)
-    second_step(1, 4, 0)
-    second_step(1, 4, 1)
+    shard_step(4, 0, 1, 2, 3, 4)
     natural(1, 4)
 
     order = (0, 2, 1)
@@ -364,6 +401,11 @@
         copy.wait_send()
     upd.wait()
     two.wait()
+
+
+def hand_over(one, two, one_out, two_out):
+    one_out[...] = one[...]
+    two_out[...] = two[...]
 
 
 def shards(stream, qkv1, w_out1, gain, w_qkv2):
@@ -416,6 +458,16 @@
         gain.reshape(4, 1, SHARE),
         stream.reshape(TOKENS, channels),
     )
+    updated, layer_two = pl.pallas_call(
+        hand_over,
+        name="outputs",
+        out_shape=(
+            jax.ShapeDtypeStruct((TOKENS, SHARE), BF),
+            jax.ShapeDtypeStruct((TOKENS, GROUP), BF),
+        ),
+        in_specs=[vmem, vmem],
+        out_specs=(vmem, vmem),
+    )(updated, layer_two.reshape(TOKENS, GROUP))
     return (
         updated.reshape(frames, tile_rows, tile_cols, SHARE),
         layer_two.reshape(frames, tile_rows, tile_cols, GROUP),

time: 114 us -> 107 us (0.939)
  local copies, waits for them, and re-layouts: 3.62 us -> 0 us
  Pallas kernels: 108 us -> 105 us
    pallas_call x1, Pallas kernels: 108 us -> 103 us  [shards(): pl.pallas_call(kernel, name='layers', out_shape=(jax.ShapeDtypeStruct((TO...]
    unnamed x2 -> x0, local copies, waits for them, and re-layouts: 3.62 us -> none
    pallas_call x0 -> x1, Pallas kernels: none -> 2.09 us  [shards(): pl.pallas_call(hand_over, name='outputs', out_shape=(jax.ShapeDtypeStruct...]
where the time goes in v3:
time: 107 us; the launch traced here: 106 us
  Pallas kernels  105 us (98%)
    pallas_call x1, Pallas kernels, shards(): pl.pallas_call(kernel, name='layers', out_shape=(jax.ShapeDtypeStruct((TO...  103 us

profile of v3, /device:TPU:1, one launch (start us, length us, event | category | flops | bytes accessed | tf_op | source)
XLA Modules:
  0.0 106.1 jit_solution(13869910992291918153)
XLA Ops:
  0.6 103.4 %layers.1 = (bf16[384,768]{1,0:T(8,128)(2,1)}, bf16[2,2,2,48,384]{4,3,2,1,0:T(8,128)(2,1)}) custom-call(bf16[16,3,24,384]{3,2,1,0:T(8,128)(2,1)} %bitcast.10, bf16[24,384]{1,0:T(8,128)(2,1)} %wo.1, bf16[3,24,384]{2,1,0:T(8,128)(2,1)} %bitcast.12, f32[4,1,768]{2,1,0:T(1,128)} %bitcast.13, bf16[384,3072]{1,0:T(8,128)(2,1)} %bitcast.9), custom_call_target="tpu_custom_call" | custom-call | tf_op jit(solution)/shard_map/layers/pallas_call | solution.py:415
  104.0 2.1 %outputs.1 = (bf16[384,768]{1,0:T(8,128)(2,1)}, bf16[384,384]{1,0:T(8,128)(2,1)}) custom-call(bf16[384,768]{1,0:T(8,128)(2,1)} %get-tuple-element.6.one, bf16[384,384]{1,0:T(8,128)(2,1)} %bitcast.11), custom_call_target="tpu_custom_call" | custom-call | tf_op jit(solution)/shard_map/outputs/pallas_call | solution.py:461

commit v4 on v3

--- a/solution.py
+++ b/solution.py
@@ -12,7 +12,7 @@
 SHARE = 768
 GROUP = 384
 WIDE = 1152
-CHUNKS = 2
+CHUNKS = 4
 PART = TOKENS // CHUNKS
 BF = jnp.bfloat16
 F32 = jnp.float32
@@ -47,7 +47,7 @@
 
 def kernel(
     qkv, wo, wq, gain, stream, upd_out, two_out,
-    own, other, line, ga, gb, w1, w2, x1, l1f, l1, ps, pr, xf, st, ub, nb, pj, hq, x2, o2, ob, lb,
+    own, other, line, ga, gb, w1, w2, x1, l1f, l1, ps, pr, xf, st, ub, nb, pj, hq, x2, o2, ob, lb, lr,
     ssem, rsem, lsem,
 ):
     row = lax.axis_index("row")
@@ -251,15 +251,15 @@
     shard_start(2)
     attend_one(1)
     first_step(3)
+    slab_step(1)
     shard_start(3)
-    slab_step(1)
     first_step(4)
-    shard_start(4)
     shard_step(1, 0)
     attend_one(2)
     l1[xh] = l1f[...].reshape(TOKENS, GROUP).astype(BF)
     send(l1.at[xh], l1.at[xh], LAYER_ONE, x_dev)
     slab_step(2)
+    shard_start(4)
     natural(0, 1)
     shard_step(1, 1, 2)
     slab_step(3)
@@ -326,13 +326,17 @@
     natural(1, 1)
     shard_step(2, 2, 3, 4)
     relay(0)
+    relay(1)
     natural(1, 2)
     shard_step(3, 0, 1)
-    relay(1)
+    relay(2)
+    relay(3)
     norm(0)
+    norm(1)
     shard_step(3, 2, 3)
-    norm(1)
+    norm(2)
     shard_step(3, 4)
+    norm(3)
     natural(1, 3)
     shard_step(4, 0, 1, 2, 3, 4)
     natural(1, 4)
@@ -383,19 +387,19 @@
             at = (fh * 2 + f) * 4 + rh * 2
             return o2[h, at : at + 2].reshape(48, HDIM).astype(BF)
 
-        lanes = pl.ds(h * HDIM, HDIM)
         for i, (fh, rh) in enumerate(quarters(a)):
             for f in range(2):
                 ob[h, fh, f, rh] = result(1 - fh, f, 1 - rh)
-            send(ob.at[h, fh, :, rh], lb.at[fh, :, rh, :, lanes], BACK + h * 3 + i, source[i])
+            send(ob.at[h, fh, :, rh], lb.at[h, fh, :, rh], BACK + h * 3 + i, source[i])
         for f in range(2):
-            lb[a, f, a, :, lanes] = result(1 - a, f, 1 - a)
+            lb[h, a, f, a] = result(1 - a, f, 1 - a)
     for h in order:
         a = sides[h]
         to = lower if a else upper
         for i, (fh, rh) in enumerate(quarters(a)):
-            arrive(lb.at[fh, :, rh, :, pl.ds(h * HDIM, HDIM)], BACK + h * 3 + i, to[i])
-    two = pltpu.make_async_copy(lb, two_out, lsem.at[2])
+            arrive(lb.at[h, fh, :, rh], BACK + h * 3 + i, to[i])
+        lr[:, h * HDIM : (h + 1) * HDIM] = lb[h].reshape(TOKENS, HDIM)
+    two = pltpu.make_async_copy(lr, two_out, lsem.at[2])
     two.start()
     for copy in sent:
         copy.wait_send()
@@ -417,7 +421,7 @@
         name="layers",
         out_shape=(
             jax.ShapeDtypeStruct((TOKENS, SHARE), BF),
-            jax.ShapeDtypeStruct((2, 2, 2, 48, GROUP), BF),
+            jax.ShapeDtypeStruct((TOKENS, GROUP), BF),
         ),
         in_specs=[vmem, vmem, vmem, vmem, anywhere],
         out_specs=(anywhere, anywhere),
@@ -443,7 +447,8 @@
             pltpu.VMEM((3, 16, 24, GROUP), F32),
             pltpu.VMEM((3, 16, 24, HDIM), F32),
             pltpu.VMEM((3, 2, 2, 2, 48, HDIM), BF),
-            pltpu.VMEM((2, 2, 2, 48, GROUP), BF),
+            pltpu.VMEM((3, 2, 2, 2, 48, HDIM), BF),
+            pltpu.VMEM((TOKENS, GROUP), BF),
             pltpu.SemaphoreType.DMA((N_SEM,)),
             pltpu.SemaphoreType.DMA((N_SEM,)),
             pltpu.SemaphoreType.DMA((3,)),
@@ -467,7 +472,7 @@
         ),
         in_specs=[vmem, vmem],
         out_specs=(vmem, vmem),
-    )(updated, layer_two.reshape(TOKENS, GROUP))
+    )(updated, layer_two)
     return (
         updated.reshape(frames, tile_rows, tile_cols, SHARE),
         layer_two.reshape(frames, tile_rows, tile_cols, GROUP),

time: 107 us -> 107 us (level)
  no operation moved by 1% of the time
where the time goes in v4:
time: 107 us; the launch traced here: 106 us
  Pallas kernels  106 us (99%)
    pallas_call x1, Pallas kernels, shards(): pl.pallas_call(kernel, name='layers', out_shape=(jax.ShapeDtypeStruct((TO...  103 us

profile of v4, /device:TPU:1, one launch (start us, length us, event | category | flops | bytes accessed | tf_op | source)
XLA Modules:
  0.0 106.2 jit_solution(16767781241177838020)
XLA Ops:
  0.6 103.5 %layers.1 = (bf16[384,768]{1,0:T(8,128)(2,1)}, bf16[384,384]{1,0:T(8,128)(2,1)}) custom-call(bf16[16,3,24,384]{3,2,1,0:T(8,128)(2,1)} %bitcast.9, bf16[24,384]{1,0:T(8,128)(2,1)} %wo.1, bf16[3,24,384]{2,1,0:T(8,128)(2,1)} %bitcast.10, f32[4,1,768]{2,1,0:T(1,128)} %bitcast.11, bf16[384,3072]{1,0:T(8,128)(2,1)} %bitcast.8), custom_call_target="tpu_custom_call" | custom-call | tf_op jit(solution)/shard_map/layers/pallas_call | solution.py:419
  104.1 2.1 %outputs.1 = (bf16[384,768]{1,0:T(8,128)(2,1)}, bf16[384,384]{1,0:T(8,128)(2,1)}) custom-call(bf16[384,768]{1,0:T(8,128)(2,1)} %get-tuple-element.6.one, bf16[384,384]{1,0:T(8,128)(2,1)} %get-tuple-element.7.two), custom_call_target="tpu_custom_call" | custom-call | tf_op jit(solution)/shard_map/outputs/pallas_call | solution.py:466
